TPU v7x, 32 devices: a whole 2x2x4 slice. The times are simulated.
32 devices in a mesh: dp: 4 (over z), list: 8 (over y, x, core).
Axes of the slice: x: 2, y: 2, z: 4, core: 2. Of those that a mesh axis runs over, the one named last changes fastest.
Arguments:
- points: bfloat16 [32768, 1024], P(('dp', 'list')), may hold values from -250 to 250
- block_list: int32 [256], P(('dp', 'list')), may hold values from 0 to 3
- centroids: bfloat16 [32, 256, 1024], P('list'), may hold values from -0.5625 to 0.5625
Outputs:
- new_centroids: float32 [32, 256, 1024], P('list', None, 'dp')
- mass: float32 [32, 256], P('list')
All inputs are finite; a program needn't handle non-finite values.
Results may differ from a plain program's by a relative error of at most 0.0024.
Values may be sent and summed in bfloat16 or wider, within the bound.
A program may use at most 128 MiB of HBM per device.

v0:
```python
import jax
import jax.numpy as jnp
from jax import lax
from jax.sharding import PartitionSpec as P

D = 1024
CENTS = 256
BLK = 128
SLOT_BLK = 1
LISTS_DEV = 4


def score_blocks(arrived, centroids):
    blocked_rows, list_index = arrived
    picked_lists = centroids[list_index]
    list_scores = jnp.einsum(
        "anpd,ankd->anpk", blocked_rows, picked_lists, preferred_element_type=jnp.float32
    )
    weights = jax.nn.softmax(list_scores, axis=-1).astype(jnp.bfloat16)
    return (blocked_rows, list_index, weights)


def on_device(points, block_list, centroids):
    list_count = lax.axis_size("list")
    blocked_rows = points.reshape(list_count, SLOT_BLK, BLK, D)
    list_index = block_list.reshape(list_count, SLOT_BLK)
    arrived = (
        lax.all_to_all(blocked_rows, "list", split_axis=0, concat_axis=0, tiled=True),
        lax.all_to_all(list_index, "list", split_axis=0, concat_axis=0, tiled=True),
    )
    kept_rows, kept_lists, weights = score_blocks(arrived, centroids)
    block_count = list_count * SLOT_BLK
    flat_rows = kept_rows.reshape(block_count * BLK, D)
    flat_weights = weights.reshape(block_count, BLK, CENTS)
    flattened_lists = kept_lists.reshape(block_count)
    membership_mask = flattened_lists[:, None] == jnp.arange(LISTS_DEV, dtype=jnp.int32)[None, :]
    member_half = membership_mask.astype(jnp.bfloat16)
    spread_weights = (flat_weights[:, :, None, :] * member_half[:, None, :, None]).reshape(
        block_count * BLK, LISTS_DEV * CENTS
    )
    totals = lax.dot_general(
        spread_weights, flat_rows, (((0,), (0,)), ((), ())), preferred_element_type=jnp.float32
    ).reshape(LISTS_DEV, CENTS, D)
    block_mass = jnp.sum(flat_weights.astype(jnp.float32), axis=1)
    masses = jnp.einsum(
        "bl,bk->lk",
        membership_mask.astype(jnp.float32),
        block_mass,
        precision=lax.Precision.HIGHEST,
    )
    all_totals, all_masses = lax.psum((totals, masses), "dp")
    share_width = D // lax.axis_size("dp")
    offset = lax.axis_index("dp") * share_width
    share_totals = lax.dynamic_slice_in_dim(all_totals, offset, share_width, 2)
    new_centroids = share_totals / jnp.maximum(all_masses, 1.0)[..., None]
    return (new_centroids, all_masses)


def solution(mesh):
    placed = (P(("dp", "list"), None), P(("dp", "list")), P("list", None, None))
    return jax.shard_map(
        on_device,
        mesh=mesh,
        in_specs=placed,
        out_specs=(P("list", None, "dp"), P("list", None)),
        check_vma=False,
    )
```

profile of v0, /device:TPU:1, one launch (start us, length us, event | category | flops | bytes accessed | tf_op | source)
XLA Modules:
  0.0 223.6 jit_solution(6219379011003440710)
XLA Ops:
  7.2 0.0 copy-start
  7.2 0.9 copy.8
  8.1 9.0 %all_to_all.14 = s32[8,1,1]{2,1,0:T(1,128)S(1)} all-to-all(s32[8,1,1]{2,1,0:T(1,128)S(1)} %copy.8), channel_id=1, replica_groups=mesh['dp'=4,'list'=8] {'list'}, dimensions={0} | all-to-all | bytes 64 | tf_op jit(solution)/shard_map/all_to_all | solution.py:29
  17.0 4.9 %all-to-all-start.1 = ((bf16[8,1,128,1024]{3,2,1,0:T(8,128)(2,1)}), bf16[8,1,128,1024]{3,2,1,0:T(8,128)(2,1)}, u32[]{:S(2)}, u32[]{:S(2)}) async-start(bf16[8,1,128,1024]{3,2,1,0:T(8,128)(2,1)} %bitcast.31), calls=%async_computation.1 | async-start | bytes 4194304 | tf_op jit(solution)/shard_map/all_to_all | solution.py:28
  21.9 0.0 all-reduce.2.cloned.1.call-start
  21.9 0.4 fusion.8
  22.3 0.0 copy-done
  22.4 2.7 %gather_fusion = bf16[8,256,1024]{2,1,0:T(8,128)(2,1)} fusion(bf16[4,256,1024]{2,1,0:T(8,128)(2,1)S(1)} %copy-done, s32[1024]{0:T(1024)S(1)} %pad_clamp_fusion), kind=kCustom, calls=%fused_computation | custom fusion | bytes 8388640 | tf_op jit(solution)/shard_map/gather | solution.py:15
  25.1 20.0 %all-to-all-done.1 = bf16[8,1,128,1024]{3,2,1,0:T(8,128)(2,1)} async-done(((bf16[8,1,128,1024]{3,2,1,0:T(8,128)(2,1)}), bf16[8,1,128,1024]{3,2,1,0:T(8,128)(2,1)}, u32[]{:S(2)}, u32[]{:S(2)}) %all-to-all-start.1) | async-done | bytes 2097184 | tf_op jit(solution)/shard_map/all_to_all | solution.py:28
  45.1 4.2 %fusion.12 = (f32[8,128]{1,0:T(8,128)S(1)}, f32[8,128,256]{1,2,0:T(8,128)S(1)}) fusion(bf16[8,256,1024]{2,1,0:T(8,128)(2,1)} %gather_fusion, bf16[8,1,128,1024]{3,2,1,0:T(8,128)(2,1)} %all-to-all-done.1), kind=kOutput, calls=%fused_computation.20 | convolution fusion | flops 537395456 | bytes 7344128 | tf_op jit(solution)/shard_map/sub | solution.py:19
  49.3 0.4 convert_reduce_fusion
  49.6 0.3 copy.9
  50.0 0.2 broadcast_multiply_fusion
  50.2 0.6 copy.12
  50.9 5.9 %fusion.15 = f32[4,256,1024]{2,1,0:T(8,128)} fusion(bf16[4,256,1024]{2,1,0:T(8,128)(2,1)S(1)} %bitcast.32, bf16[1024,1024,1]{1,0,2:T(8,128)(2,1)} %bitcast.7), kind=kOutput, calls=%fused_computation.21 | convolution fusion | flops 2147483648 | bytes 8388608 | tf_op jit(solution)/shard_map/dot_general | solution.py:41
  56.7 0.0 all-reduce.2.cloned.1.call-update
  56.8 0.1 fusion.9
  56.9 10.2 %psum.15 = f32[4,256]{1,0:T(4,128)S(1)} all-reduce(f32[4,256]{1,0:T(4,128)S(1)} %fusion.9), channel_id=1, replica_groups=mesh['dp'=4,'list'=8] {'dp'}, use_global_device_ids=true, to_apply=%region_4.0 | all-reduce | flops 1024 | bytes 8192 | tf_op jit(solution)/shard_map/psum | solution.py:51
  67.1 0.0 copy-start.1
  67.1 147.2 %all-reduce.2.cloned.1.call-done = f32[4,256,1024]{2,1,0:T(8,128)} async-done(((f32[4,256,1024]{2,1,0:T(8,128)}), f32[4,256,1024]{2,1,0:T(8,128)}) %all-reduce.2.cloned.1.call-update) | async-done | bytes 4194320 | tf_op jit(solution)/shard_map/psum | solution.py:51
  214.3 2.4 %dynamic-slice_divide_fusion = f32[4,256,256]{2,1,0:T(8,128)} fusion(f32[4,256,1024]{2,1,0:T(8,128)} %all-reduce.2.cloned.1.call-done, s32[]{:T(128)S(6)} %select_n.10, f32[4,256]{1,0:T(4,128)S(1)} %broadcast_maximum_fusion), kind=kLoop, calls=%fused_computation.9 | loop fusion | flops 262144 | bytes 2101252 | tf_op jit(solution)/shard_map/div | solution.py:55
  216.7 0.0 copy-done.1
  (3 shorter events, 0.0 us)
Async XLA Ops:
  7.2 15.2 %copy-start = (bf16[4,256,1024]{2,1,0:T(8,128)(2,1)S(1)}, bf16[4,256,1024]{2,1,0:T(8,128)(2,1)}, u32[]{:S(2)}) copy-start(bf16[4,256,1024]{2,1,0:T(8,128)(2,1)} %param.5) | copy-start | bytes 6291460
  17.0 28.1 %all-to-all-start.1 = ((bf16[8,1,128,1024]{3,2,1,0:T(8,128)(2,1)}), bf16[8,1,128,1024]{3,2,1,0:T(8,128)(2,1)}, u32[]{:S(2)}, u32[]{:S(2)}) async-start(bf16[8,1,128,1024]{3,2,1,0:T(8,128)(2,1)} %bitcast.31), calls=%async_computation.1 | async-start | bytes 4194304 | tf_op jit(solution)/shard_map/all_to_all | solution.py:28
  21.9 192.4 %all-reduce.2.cloned.1.call-start = ((), (), s32[]{:S(2)}) async-start(), calls=%async_computation.2 | async-start | bytes 8388608 | tf_op jit(solution)/shard_map/psum | solution.py:51
  67.1 149.6 %copy-start.1 = (f32[4,256]{1,0:T(4,128)}, f32[4,256]{1,0:T(4,128)S(1)}, u32[]{:S(2)}) copy-start(f32[4,256]{1,0:T(4,128)S(1)} %psum.15) | copy-start | bytes 12292
Sparse Core Ops, SparseCore 0:
  56.9 157.3 all-reduce.1
where the time goes:
time: 224 us
  waiting for transfers between devices  167 us (75%)
  blocking collectives  19.2 us (9%)
  between operations  14.1 us (6%)
  matrix products  10.2 us (5%)
  starting transfers between devices  4.91 us (2%)
  local copies, waits for them, and re-layouts  4.6 us (2%)
  other arithmetic  3.4 us (2%)
    psum x1, waiting for transfers between devices, on_device(): all_totals, all_masses = lax.psum((totals, masses), 'dp')  147 us
    all_to_all x1, waiting for transfers between devices, on_device(): lax.all_to_all(blocked_rows, 'list', split_axis=0, concat_axis=0, tiled=T...  20 us
    psum x1, blocking collectives, on_device(): all_totals, all_masses = lax.psum((totals, masses), 'dp')  10.2 us
    all_to_all x1, blocking collectives, on_device(): lax.all_to_all(list_index, 'list', split_axis=0, concat_axis=0, tiled=True)  8.97 us
    dot_general x1, matrix products, on_device(): lax.dot_general(spread_weights, flat_rows, (((0,), (0,)), ((), ())), pref...  5.85 us
    all_to_all x1, starting transfers between devices, on_device(): lax.all_to_all(blocked_rows, 'list', split_axis=0, concat_axis=0, tiled=T...  4.91 us
  transfers between devices with their start and end apart: 2, of which 2 were waited for; matrix products, arithmetic and copies ran while one was open for 1% of the time, Pallas kernels for 0%

commit v1 on v0

v1 whole, which is shorter than its diff:
```python
import functools

import jax
import jax.numpy as jnp
from jax import lax
from jax.experimental import pallas as pl
from jax.experimental.pallas import tpu as pltpu
from jax.sharding import PartitionSpec as P

D = 1024
CENTS = 256
BLK = 128
LISTS_DEV = 4
ROWS = LISTS_DEV * CENTS
SPLIT = 2
PART = ROWS // SPLIT
MESH = pl.DeviceIdType.MESH


def exclusive_or(a, b):
    result, bit = 0, 1
    while bit <= b:
        if b & bit:
            result = result + bit - 2 * bit * ((a // bit) % 2)
        bit *= 2
    return a + result


def kernel(
    n, dps, share,
    points, block_list, centroids, totals, mass,
    cents, arrived, list_out, list_in, wts,
    direct_out, far_out, near_in, merge_in, far_in, own_far, mass_out, mass_in,
    local_sem, row_send, row_recv, list_send, list_recv,
    direct_send, far_send, near_recv, merge_recv, far_recv, mass_send, mass_recv,
):
    me = lax.axis_index("list")
    dp = lax.axis_index("dp")
    core = me % 2
    pairs = dps // 2

    cent_copy = pltpu.make_async_copy(centroids, cents, local_sem.at[0])
    cent_copy.start()
    own_copy = pltpu.make_async_copy(points.at[me], arrived.at[0], local_sem.at[1])
    own_copy.start()

    barrier = pltpu.get_barrier_semaphore()
    for k in range(1, n):
        pl.semaphore_signal(barrier, inc=1, device_id={"list": exclusive_or(me, k)}, device_id_type=MESH)
    for k in range(1, dps):
        pl.semaphore_signal(barrier, inc=1, device_id={"dp": (dp + k) % dps}, device_id_type=MESH)
    for o in range(n):
        list_out[o] = jnp.full((1, BLK), block_list[o], jnp.int32)
    list_in[0] = jnp.full((1, BLK), block_list[me], jnp.int32)
    pl.semaphore_wait(barrier, n - 1 + dps - 1)

    def row_copy(i, u):
        k = 2 * i + u
        owner = 2 * exclusive_or(me // 2, i) + (core + u) % 2
        return pltpu.make_async_remote_copy(
            src_ref=points.at[owner], dst_ref=arrived.at[k],
            send_sem=row_send.at[k], recv_sem=row_recv.at[k],
            device_id={"list": owner}, device_id_type=MESH,
        )

    def list_copy(i, u):
        k = 2 * i + u
        owner = 2 * exclusive_or(me // 2, i) + (core + u) % 2
        return pltpu.make_async_remote_copy(
            src_ref=list_out.at[owner], dst_ref=list_in.at[k],
            send_sem=list_send.at[k], recv_sem=list_recv.at[k],
            device_id={"list": owner}, device_id_type=MESH,
        )

    chip_order = list(range(n // 2 - 1, 0, -1))
    for i in range(n // 2):
        for u in range(2):
            if i or u:
                list_copy(i, u).start()
    row_copy(0, 1).start()
    for i in chip_order:
        row_copy(i, core).start()
    for i in chip_order:
        row_copy(i, core).wait_send()
    for i in chip_order:
        row_copy(i, (core + 1) % 2).start()

    def score(k):
        rows = arrived[k]
        lists = list_in[k]
        member = [lists == l for l in range(LISTS_DEV)]
        picked = None
        for l in reversed(range(LISTS_DEV)):
            s = lax.dot_general(cents[l], rows, (((1,), (1,)), ((), ())), preferred_element_type=jnp.float32)
            picked = s if picked is None else jnp.where(member[l], s, picked)
        e = jnp.exp(picked - jnp.max(picked, axis=0, keepdims=True))
        w = e / jnp.sum(e, axis=0, keepdims=True)
        columns = pl.ds(pl.multiple_of(k * BLK, BLK), BLK)
        for l in range(LISTS_DEV):
            wts[l * CENTS:(l + 1) * CENTS, columns] = jnp.where(member[l], w, 0.0).astype(jnp.bfloat16)

    cent_copy.wait()
    own_copy.wait()
    score(0)

    def visit(k, carry):
        i, u = k // 2, k % 2
        pltpu.make_async_remote_copy(
            src_ref=list_out.at[0], dst_ref=list_in.at[k], send_sem=list_send.at[k],
            recv_sem=list_recv.at[k], device_id={"list": me}, device_id_type=MESH,
        ).wait_recv()
        pltpu.make_async_remote_copy(
            src_ref=points.at[0], dst_ref=arrived.at[k], send_sem=row_send.at[k],
            recv_sem=row_recv.at[k], device_id={"list": me}, device_id_type=MESH,
        ).wait_recv()
        score(k)
        return carry

    lax.fori_loop(1, n, visit, 0)

    def partial(d, r):
        columns = pl.ds(pl.multiple_of(d * share, 128), share)
        feats = arrived[:, :, columns].reshape(n * BLK, share)
        return jnp.dot(wts[r * PART:(r + 1) * PART, :], feats, preferred_element_type=jnp.float32)

    partner = dp + 1 - 2 * (dp % 2)
    pair = dp // 2

    def direct_copy(r):
        return pltpu.make_async_remote_copy(
            src_ref=direct_out.at[r], dst_ref=near_in.at[r],
            send_sem=direct_send.at[r], recv_sem=near_recv.at[r],
            device_id={"dp": partner}, device_id_type=MESH,
        )

    def send_direct():
        for r in range(SPLIT):
            direct_out[r] = partial(partner, r).astype(jnp.bfloat16)
            direct_copy(r).start()

    def merge_copy(slot):
        return pltpu.make_async_remote_copy(
            src_ref=far_out.at[slot], dst_ref=merge_in.at[slot],
            send_sem=far_send.at[slot], recv_sem=merge_recv.at[slot],
            device_id={"dp": partner}, device_id_type=MESH,
        )

    def far_copy(slot, dest, landing):
        return pltpu.make_async_remote_copy(
            src_ref=far_out.at[slot], dst_ref=far_in.at[landing],
            send_sem=far_send.at[slot], recv_sem=far_recv.at[landing],
            device_id={"dp": dest}, device_id_type=MESH,
        )

    def mass_copy(k):
        return pltpu.make_async_remote_copy(
            src_ref=mass_out, dst_ref=mass_in.at[k - 1],
            send_sem=mass_send.at[k - 1], recv_sem=mass_recv.at[k - 1],
            device_id={"dp": (dp + k) % dps}, device_id_type=MESH,
        )

    for j in range(1, pairs):
        other = (pair + j) % pairs
        right = (other > pair).astype(jnp.int32)
        outer = (dp + right) % 2 == 1

        @pl.when(outer)
        def _():
            for m in range(2):
                dest = 2 * other + (right + m) % 2
                for r in range(SPLIT):
                    slot = ((j - 1) * 2 + m) * SPLIT + r
                    far_out[slot] = partial(dest, r).astype(jnp.bfloat16)
                    merge_copy(slot).start()

    send_direct()

    lane_mass = lax.dot_general(
        jnp.ones((8, n * BLK), jnp.bfloat16), wts[...], (((1,), (1,)), ((), ())),
        preferred_element_type=jnp.float32,
    )
    for r in range(8):
        mass_out[r:r + 1, :] = lane_mass[r:r + 1, r * 128:(r + 1) * 128]
    for k in range(1, dps):
        mass_copy(k).start()

    for j in range(1, pairs):
        other = (pair + j) % pairs
        right = (other > pair).astype(jnp.int32)
        outer = (dp + right) % 2 == 1

        @pl.when(jnp.logical_not(outer))
        def _():
            for m in range(2):
                dest = 2 * other + (right + m) % 2
                for r in range(SPLIT):
                    own_far[m * SPLIT + r] = partial(dest, r)
            for m in range(2):
                dest = 2 * other + (right + m) % 2
                for r in range(SPLIT):
                    slot = ((j - 1) * 2 + m) * SPLIT + r
                    merge_copy(slot).wait_recv()
                    far_out[slot] = (own_far[m * SPLIT + r] + merge_in[slot].astype(jnp.float32)).astype(jnp.bfloat16)
                    far_copy(slot, dest, (j - 1) * SPLIT + r).start()

    for r in range(SPLIT):
        totals[r * PART:(r + 1) * PART, :] = partial(dp, r)
    for r in range(SPLIT):
        direct_copy(r).wait_recv()
        totals[r * PART:(r + 1) * PART, :] += near_in[r].astype(jnp.float32)
    whole_mass = mass_out[...]
    for k in range(1, dps):
        mass_copy(k).wait_recv()
        whole_mass = whole_mass + mass_in[k - 1]
    mass[...] = whole_mass
    for j in range(1, pairs):
        for r in range(SPLIT):
            landing = (j - 1) * SPLIT + r
            far_copy(landing, partner, landing).wait_recv()
            totals[r * PART:(r + 1) * PART, :] += far_in[landing].astype(jnp.float32)

    for i in range(n // 2):
        for u in range(2):
            if i or u:
                list_copy(i, u).wait_send()
    row_copy(0, 1).wait_send()
    for i in chip_order:
        row_copy(i, (core + 1) % 2).wait_send()
    for r in range(SPLIT):
        direct_copy(r).wait_send()
    for slot in range((pairs - 1) * 2 * SPLIT):
        merge_copy(slot).wait_send()
    for k in range(1, dps):
        mass_copy(k).wait_send()


def on_device(points, block_list, centroids):
    n = lax.axis_size("list")
    dps = lax.axis_size("dp")
    share = D // dps
    pairs = dps // 2
    far = max((pairs - 1) * SPLIT, 1)
    dma = pltpu.SemaphoreType.DMA
    half, single = jnp.bfloat16, jnp.float32
    totals, mass = pl.pallas_call(
        functools.partial(kernel, n, dps, share),
        out_shape=(
            jax.ShapeDtypeStruct((ROWS, share), single),
            jax.ShapeDtypeStruct((8, 128), single),
        ),
        in_specs=[
            pl.BlockSpec(memory_space=pl.ANY),
            pl.BlockSpec(memory_space=pltpu.SMEM),
            pl.BlockSpec(memory_space=pl.ANY),
        ],
        out_specs=(
            pl.BlockSpec(memory_space=pltpu.VMEM),
            pl.BlockSpec(memory_space=pltpu.VMEM),
        ),
        scratch_shapes=[
            pltpu.VMEM((LISTS_DEV, CENTS, D), half),
            pltpu.VMEM((n, BLK, D), half),
            pltpu.VMEM((n, 1, BLK), jnp.int32),
            pltpu.VMEM((n, 1, BLK), jnp.int32),
            pltpu.VMEM((ROWS, n * BLK), half),
            pltpu.VMEM((SPLIT, PART, share), half),
            pltpu.VMEM((2 * far, PART, share), half),
            pltpu.VMEM((SPLIT, PART, share), half),
            pltpu.VMEM((2 * far, PART, share), half),
            pltpu.VMEM((far, PART, share), half),
            pltpu.VMEM((2 * SPLIT, PART, share), single),
            pltpu.VMEM((8, 128), single),
            pltpu.VMEM((dps - 1, 8, 128), single),
            dma((2,)), dma((n,)), dma((n,)), dma((n,)), dma((n,)),
            dma((SPLIT,)), dma((2 * far,)), dma((SPLIT,)), dma((2 * far,)), dma((far,)),
            dma((dps - 1,)), dma((dps - 1,)),
        ],
        compiler_params=pltpu.CompilerParams(
            collective_id=0, has_side_effects=True, vmem_limit_bytes=56 * 1024 * 1024,
        ),
        cost_estimate=pl.CostEstimate(flops=4 * 2 * n * BLK * CENTS * D * 2, bytes_accessed=8 << 20, transcendentals=n * BLK * CENTS),
    )(points.reshape(n, BLK, D), block_list, centroids)
    mass = mass.reshape(LISTS_DEV, CENTS)
    new_centroids = totals.reshape(LISTS_DEV, CENTS, share) / jnp.maximum(mass, 1.0)[..., None]
    return new_centroids, mass


def solution(mesh):
    placed = (P(("dp", "list"), None), P(("dp", "list")), P("list", None, None))
    return jax.shard_map(
        on_device,
        mesh=mesh,
        in_specs=placed,
        out_specs=(P("list", None, "dp"), P("list", None)),
        check_vma=False,
    )
```

time: 224 us -> 68.1 us (0.30)
  waiting for transfers between devices: 167 us -> 0 us
  Pallas kernels: 0 us -> 64.2 us
  blocking collectives: 19.2 us -> 0 us
  between operations: 14.1 us -> 0.64 us
  matrix products: 10.2 us -> 0 us
  starting transfers between devices: 4.91 us -> 0 us
  local copies, waits for them, and re-layouts: 4.6 us -> 0.68 us
    psum x1 -> x0, waiting for transfers between devices: 147 us -> none  [on_device(): all_totals, all_masses = lax.psum((totals, masses), 'dp')]
    pallas_call x0 -> x1, Pallas kernels: none -> 64.2 us  [on_device(): pl.pallas_call(functools.partial(kernel, n, dps, share), out_shape=(jax.S...]
    all_to_all x1 -> x0, waiting for transfers between devices: 20 us -> none  [on_device(): lax.all_to_all(blocked_rows, 'list', split_axis=0, concat_axis=0, tiled=T...]
    psum x1 -> x0, blocking collectives: 10.2 us -> none  [on_device(): all_totals, all_masses = lax.psum((totals, masses), 'dp')]
    all_to_all x1 -> x0, blocking collectives: 8.97 us -> none  [on_device(): lax.all_to_all(list_index, 'list', split_axis=0, concat_axis=0, tiled=True)]
    dot_general x2 -> x0, matrix products: 5.97 us -> none  [the longest x1 5.85 us: on_device(): lax.dot_general(spread_weights, flat_rows, (((0,), (0,)), ((), ())), pref...]
    all_to_all x1 -> x0, starting transfers between devices: 4.91 us -> none  [on_device(): lax.all_to_all(blocked_rows, 'list', split_axis=0, concat_axis=0, tiled=T...]
    sub x1 -> x0, matrix products: 4.2 us -> none  [score_blocks(): weights = jax.nn.softmax(list_scores, axis=-1).astype(jnp.bfloat16)]
  transfers between devices with their start and end apart: 2 -> 0, of which waited for: 2 -> 0; matrix products, arithmetic and copies ran while one was open for 1% -> 0% of each run, Pallas kernels for 0% -> 0%
where the time goes in v1:
time: 68.1 us; the launch traced here: 68 us
  Pallas kernels  64.2 us (94%)
  other arithmetic  2.41 us (4%)
    pallas_call x1, Pallas kernels, on_device(): pl.pallas_call(functools.partial(kernel, n, dps, share), out_shape=(jax.S...  64.2 us
    div x1, other arithmetic, on_device(): totals.reshape(LISTS_DEV, CENTS, share) / jnp.maximum(mass, 1.0)[..., None]  2.4 us

profile of v1, /device:TPU:1, one launch (start us, length us, event | category | flops | bytes accessed | tf_op | source)
XLA Modules:
  0.0 68.0 jit_solution(9940669476460958762)
XLA Ops:
  0.6 64.2 %shard_map.50 = (f32[1024,256]{1,0:T(8,128)}, f32[8,128]{1,0:T(8,128)}) custom-call(bf16[8,128,1024]{2,1,0:T(8,128)(2,1)} %bitcast.3, s32[8]{0:T(128)} %block_list.1, bf16[4,256,1024]{2,1,0:T(8,128)(2,1)} %centroids.1), custom_call_target="tpu_custom_call" | custom-call | flops 4294967296 | bytes 8388608 | tf_op jit(solution)/shard_map/pallas_call | solution.py:245
  64.9 0.7 %reshape.20 = f32[4,256]{1,0:T(4,128)S(1)} reshape(f32[8,128]{1,0:T(8,128)} %get-tuple-element.5) | data formatting | bytes 8192 | tf_op jit(solution)/shard_map/reshape | solution.py:283
  65.5 0.0 copy-start
  65.6 2.4 %broadcast_divide_fusion = f32[4,256,256]{2,1,0:T(8,128)} fusion(f32[4,256,256]{2,1,0:T(8,128)} %bitcast.2, f32[4,256]{1,0:T(4,128)S(1)} %broadcast_maximum_fusion), kind=kLoop, calls=%fused_computation | loop fusion | flops 262144 | bytes 2101248 | tf_op jit(solution)/shard_map/div | solution.py:284
  68.0 0.0 copy-done
  (1 shorter events, 0.0 us)
Async XLA Ops:
  65.5 2.4 %copy-start = (f32[4,256]{1,0:T(4,128)}, f32[4,256]{1,0:T(4,128)S(1)}, u32[]{:S(2)}) copy-start(f32[4,256]{1,0:T(4,128)S(1)} %reshape.20) | copy-start | bytes 12292

commit v2 on v1

v2 whole, which is shorter than its diff:
```python
import functools

import jax
import jax.numpy as jnp
from jax import lax
from jax.experimental import pallas as pl
from jax.experimental.pallas import tpu as pltpu
from jax.sharding import PartitionSpec as P

D = 1024
CENTS = 256
BLK = 128
LISTS_DEV = 4
ROWS = LISTS_DEV * CENTS
SPLIT = 2
PART = ROWS // SPLIT
MESH = pl.DeviceIdType.MESH


def exclusive_or(a, b):
    result, bit = 0, 1
    while bit <= b:
        if b & bit:
            result = result + bit - 2 * bit * ((a // bit) % 2)
        bit *= 2
    return a + result


def kernel(
    n, dps, share,
    points, block_list, centroids, totals, mass,
    cents, arrived, list_out, list_in, wts,
    direct_out, far_out, near_in, merge_in, far_in, own_far, mass_out, mass_in,
    local_sem, row_send, row_recv, list_send, list_recv,
    direct_send, far_send, near_recv, merge_recv, far_recv, mass_send, mass_recv,
):
    me = lax.axis_index("list")
    dp = lax.axis_index("dp")
    core, chip = me % 2, me // 2
    chips = n // 2
    pairs = dps // 2
    pair = dp // 2
    partner = dp + 1 - 2 * (dp % 2)

    def home_of(p):
        return 2 * p + (2 * p < pairs).astype(jnp.int32)

    home = home_of(pair)
    away = (dp != home).astype(jnp.int32)
    even = core == 0
    gathers = (core == 1) & (away == 0)
    idle = (core == 1) & (away == 1)

    cent_copy = pltpu.make_async_copy(centroids, cents, local_sem.at[0])
    cent_copy.start()
    own_copy = pltpu.make_async_copy(points.at[me], arrived.at[0], local_sem.at[1])

    @pl.when(jnp.logical_not(idle))
    def _():
        own_copy.start()

    barrier = pltpu.get_barrier_semaphore()
    for k in range(1, n):
        peer = exclusive_or(me, k)
        pl.semaphore_signal(barrier, inc=1, device_id={"dp": dp, "list": peer}, device_id_type=MESH)
        pl.semaphore_signal(barrier, inc=1, device_id={"dp": partner, "list": peer}, device_id_type=MESH)
    for k in range(1, dps):
        pl.semaphore_signal(barrier, inc=1, device_id={"dp": (dp + k) % dps, "list": me}, device_id_type=MESH)
    for o in range(n):
        list_out[o] = jnp.full((1, BLK), block_list[o], jnp.int32)
    list_in[0] = jnp.full((1, BLK), block_list[me], jnp.int32)
    pl.semaphore_wait(barrier, 2 * (n - 1) + dps - 1)

    def route(i, odd):
        k = 2 * i + (core + odd) % 2
        owner = 2 * exclusive_or(chip, i) + odd
        target = dp + odd * (home - dp)
        return k, owner, target, k + n * odd * away

    def row_copy(i, odd):
        k, owner, target, slot = route(i, odd)
        return pltpu.make_async_remote_copy(
            src_ref=points.at[owner], dst_ref=arrived.at[slot],
            send_sem=row_send.at[k], recv_sem=row_recv.at[slot],
            device_id={"dp": target, "list": owner}, device_id_type=MESH,
        )

    def list_copy(i, odd):
        k, owner, target, slot = route(i, odd)
        return pltpu.make_async_remote_copy(
            src_ref=list_out.at[owner], dst_ref=list_in.at[slot],
            send_sem=list_send.at[k], recv_sem=list_recv.at[slot],
            device_id={"dp": target, "list": owner}, device_id_type=MESH,
        )

    def each_route(act):
        for i in range(chips):
            for odd in (away, 1 - away):
                if i:
                    act(i, odd)
                else:
                    @pl.when((core != odd) | (odd * away == 1))
                    def _():
                        act(i, odd)

    each_route(lambda i, odd: list_copy(i, odd).start())
    each_route(lambda i, odd: row_copy(i, odd).start())

    def score(batch):
        rows = arrived[pl.ds(2 * batch, 2)].reshape(2 * BLK, D)
        lists = jnp.concatenate([list_in[2 * batch], list_in[2 * batch + 1]], axis=1)
        member = [lists == l for l in range(LISTS_DEV)]
        picked = None
        for l in reversed(range(LISTS_DEV)):
            s = lax.dot_general(cents[l], rows, (((1,), (1,)), ((), ())), preferred_element_type=jnp.float32)
            picked = s if picked is None else jnp.where(member[l], s, picked)
        e = jnp.exp(picked - jnp.max(picked, axis=0, keepdims=True))
        w = e / jnp.sum(e, axis=0, keepdims=True)
        columns = pl.ds(pl.multiple_of(batch * 2 * BLK, 2 * BLK), 2 * BLK)
        for l in range(LISTS_DEV):
            wts[l * CENTS:(l + 1) * CENTS, columns] = jnp.where(member[l], w, 0.0).astype(jnp.bfloat16)

    def landed(slot):
        pltpu.make_async_remote_copy(
            src_ref=list_out.at[0], dst_ref=list_in.at[slot], send_sem=list_send.at[0],
            recv_sem=list_recv.at[slot], device_id={"dp": dp, "list": me}, device_id_type=MESH,
        ).wait_recv()
        pltpu.make_async_remote_copy(
            src_ref=points.at[0], dst_ref=arrived.at[slot], send_sem=row_send.at[0],
            recv_sem=row_recv.at[slot], device_id={"dp": dp, "list": me}, device_id_type=MESH,
        ).wait_recv()

    cent_copy.wait()

    @pl.when(jnp.logical_not(idle))
    def _():
        own_copy.wait()
        landed(1)
        score(0)

        def visit(step, carry):
            batch = step + (core * ((step // 2) + (step % 2) * chips - step))
            landed(2 * batch)
            landed(2 * batch + 1)
            score(batch)
            return carry

        lax.fori_loop(1, chips * (1 + core), visit, 0)

    def partial(d, r, count):
        columns = pl.ds(pl.multiple_of(d * share, 128), share)
        feats = arrived[0:count, :, columns].reshape(count * BLK, share)
        return jnp.dot(
            wts[r * PART:(r + 1) * PART, 0:count * BLK], feats, preferred_element_type=jnp.float32
        )

    def direct_copy(r):
        return pltpu.make_async_remote_copy(
            src_ref=direct_out.at[r], dst_ref=near_in.at[r],
            send_sem=direct_send.at[r], recv_sem=near_recv.at[r],
            device_id={"dp": partner, "list": me}, device_id_type=MESH,
        )

    def send_direct(count):
        for r in range(SPLIT):
            direct_out[r] = partial(partner, r, count).astype(jnp.bfloat16)
            direct_copy(r).start()

    def merge_copy(slot):
        return pltpu.make_async_remote_copy(
            src_ref=far_out.at[slot], dst_ref=merge_in.at[slot],
            send_sem=far_send.at[slot], recv_sem=merge_recv.at[slot],
            device_id={"dp": partner, "list": me}, device_id_type=MESH,
        )

    def far_copy(slot, dest, landing):
        return pltpu.make_async_remote_copy(
            src_ref=far_out.at[slot], dst_ref=far_in.at[landing],
            send_sem=far_send.at[slot], recv_sem=far_recv.at[landing],
            device_id={"dp": dest, "list": me}, device_id_type=MESH,
        )

    def mass_copy(k):
        return pltpu.make_async_remote_copy(
            src_ref=mass_out, dst_ref=mass_in.at[k - 1],
            send_sem=mass_send.at[k - 1], recv_sem=mass_recv.at[k - 1],
            device_id={"dp": (dp + k) % dps, "list": me}, device_id_type=MESH,
        )

    def send_mass(count):
        lane_mass = lax.dot_general(
            jnp.ones((8, count * BLK), jnp.bfloat16), wts[:, 0:count * BLK], (((1,), (1,)), ((), ())),
            preferred_element_type=jnp.float32,
        )
        for r in range(8):
            mass_out[r:r + 1, :] = lane_mass[r:r + 1, r * 128:(r + 1) * 128]
        for k in range(1, dps):
            mass_copy(k).start()

    def others():
        for j in range(1, pairs):
            other = (pair + j) % pairs
            right = (other > pair).astype(jnp.int32)
            yield j, other, right, (dp + right) % 2 == 1

    def far_parts(j, other, right):
        for m in range(2):
            for r in range(SPLIT):
                yield 2 * other + (right + m) % 2, m, r, ((j - 1) * 2 + m) * SPLIT + r

    @pl.when(even)
    def _():
        for j, other, right, outer in others():
            @pl.when(outer)
            def _():
                for dest, m, r, slot in far_parts(j, other, right):
                    far_out[slot] = partial(dest, r, n).astype(jnp.bfloat16)
                    merge_copy(slot).start()

        send_direct(n)
        send_mass(n)

        for j, other, right, outer in others():
            @pl.when(jnp.logical_not(outer))
            def _():
                for dest, m, r, slot in far_parts(j, other, right):
                    own_far[m * SPLIT + r] = partial(dest, r, n)
                for dest, m, r, slot in far_parts(j, other, right):
                    merge_copy(slot).wait_recv()
                    far_out[slot] = (own_far[m * SPLIT + r] + merge_in[slot].astype(jnp.float32)).astype(jnp.bfloat16)
                    far_copy(slot, dest, (j - 1) * SPLIT + r).start()

        for r in range(SPLIT):
            totals[r * PART:(r + 1) * PART, :] = partial(dp, r, n)

    @pl.when(gathers)
    def _():
        for j, other, right, outer in others():
            for dest, m, r, slot in far_parts(j, other, right):
                far_out[slot] = partial(dest, r, 2 * n).astype(jnp.bfloat16)
                far_copy(slot, dest, (j - 1) * SPLIT + r).start()
        send_direct(2 * n)
        send_mass(2 * n)
        for r in range(SPLIT):
            totals[r * PART:(r + 1) * PART, :] = partial(dp, r, 2 * n)

    @pl.when(idle)
    def _():
        totals[...] = jnp.zeros_like(totals)
        mass_out[...] = jnp.zeros_like(mass_out)

    mass[...] = mass_out[...]
    for k in range(1, dps):
        sender = (dp + dps - k) % dps

        @pl.when(even | (sender == home_of(sender // 2)))
        def _():
            mass_copy(k).wait_recv()
            mass[...] += mass_in[k - 1]

    for j in range(1, pairs):
        for r in range(SPLIT):
            landing = (j - 1) * SPLIT + r
            far_copy(landing, partner, landing).wait_recv()
            totals[r * PART:(r + 1) * PART, :] += far_in[landing].astype(jnp.float32)

    @pl.when(jnp.logical_not(gathers))
    def _():
        for r in range(SPLIT):
            direct_copy(r).wait_recv()
            totals[r * PART:(r + 1) * PART, :] += near_in[r].astype(jnp.float32)

    each_route(lambda i, odd: list_copy(i, odd).wait_send())
    each_route(lambda i, odd: row_copy(i, odd).wait_send())

    @pl.when(jnp.logical_not(idle))
    def _():
        for r in range(SPLIT):
            direct_copy(r).wait_send()
        for slot in range((pairs - 1) * 2 * SPLIT):
            merge_copy(slot).wait_send()
        for k in range(1, dps):
            mass_copy(k).wait_send()


def on_device(points, block_list, centroids):
    n = lax.axis_size("list")
    dps = lax.axis_size("dp")
    share = D // dps
    pairs = dps // 2
    far = max((pairs - 1) * SPLIT, 1)
    dma = pltpu.SemaphoreType.DMA
    half, single = jnp.bfloat16, jnp.float32
    totals, mass = pl.pallas_call(
        functools.partial(kernel, n, dps, share),
        out_shape=(
            jax.ShapeDtypeStruct((ROWS, share), single),
            jax.ShapeDtypeStruct((8, 128), single),
        ),
        in_specs=[
            pl.BlockSpec(memory_space=pl.ANY),
            pl.BlockSpec(memory_space=pltpu.SMEM),
            pl.BlockSpec(memory_space=pl.ANY),
        ],
        out_specs=(
            pl.BlockSpec(memory_space=pltpu.VMEM),
            pl.BlockSpec(memory_space=pltpu.VMEM),
        ),
        scratch_shapes=[
            pltpu.VMEM((LISTS_DEV, CENTS, D), half),
            pltpu.VMEM((2 * n, BLK, D), half),
            pltpu.VMEM((n, 1, BLK), jnp.int32),
            pltpu.VMEM((2 * n, 1, BLK), jnp.int32),
            pltpu.VMEM((ROWS, 2 * n * BLK), half),
            pltpu.VMEM((SPLIT, PART, share), half),
            pltpu.VMEM((2 * far, PART, share), half),
            pltpu.VMEM((SPLIT, PART, share), half),
            pltpu.VMEM((2 * far, PART, share), half),
            pltpu.VMEM((far, PART, share), half),
            pltpu.VMEM((2 * SPLIT, PART, share), single),
            pltpu.VMEM((8, 128), single),
            pltpu.VMEM((dps - 1, 8, 128), single),
            dma((2,)), dma((n,)), dma((2 * n,)), dma((n,)), dma((2 * n,)),
            dma((SPLIT,)), dma((2 * far,)), dma((SPLIT,)), dma((2 * far,)), dma((far,)),
            dma((dps - 1,)), dma((dps - 1,)),
        ],
        compiler_params=pltpu.CompilerParams(
            collective_id=0, has_side_effects=True, vmem_limit_bytes=56 * 1024 * 1024,
        ),
        cost_estimate=pl.CostEstimate(flops=4 * 2 * n * BLK * CENTS * D * 2, bytes_accessed=8 << 20, transcendentals=n * BLK * CENTS),
    )(points.reshape(n, BLK, D), block_list, centroids)
    mass = mass.reshape(LISTS_DEV, CENTS)
    new_centroids = totals.reshape(LISTS_DEV, CENTS, share) / jnp.maximum(mass, 1.0)[..., None]
    return new_centroids, mass


def solution(mesh):
    placed = (P(("dp", "list"), None), P(("dp", "list")), P("list", None, None))
    return jax.shard_map(
        on_device,
        mesh=mesh,
        in_specs=placed,
        out_specs=(P("list", None, "dp"), P("list", None)),
        check_vma=False,
    )
```

time: 68.1 us -> 72.5 us (1.065)
  Pallas kernels: 64.2 us -> 68.6 us
    pallas_call x1, Pallas kernels: 64.2 us -> 68.6 us  [on_device(): pl.pallas_call(functools.partial(kernel, n, dps, share), out_shape=(jax.S...]
where the time goes in v2:
time: 72.5 us; the launch traced here: 72.3 us
  Pallas kernels  68.6 us (95%)
  other arithmetic  2.41 us (3%)
    pallas_call x1, Pallas kernels, on_device(): pl.pallas_call(functools.partial(kernel, n, dps, share), out_shape=(jax.S...  68.6 us
    div x1, other arithmetic, on_device(): totals.reshape(LISTS_DEV, CENTS, share) / jnp.maximum(mass, 1.0)[..., None]  2.4 us

profile of v2, /device:TPU:1, one launch (start us, length us, event | category | flops | bytes accessed | tf_op | source)
XLA Modules:
  0.0 72.3 jit_solution(7856253188868303296)
XLA Ops:
  0.6 68.6 %shard_map.50 = (f32[1024,256]{1,0:T(8,128)}, f32[8,128]{1,0:T(8,128)}) custom-call(bf16[8,128,1024]{2,1,0:T(8,128)(2,1)} %bitcast.3, s32[8]{0:T(128)} %block_list.1, bf16[4,256,1024]{2,1,0:T(8,128)(2,1)} %centroids.1), custom_call_target="tpu_custom_call" | custom-call | flops 4294967296 | bytes 8388608 | tf_op jit(solution)/shard_map/pallas_call | solution.py:294
  69.2 0.7 reshape.20
  69.9 0.0 copy-start
  69.9 2.4 %broadcast_divide_fusion = f32[4,256,256]{2,1,0:T(8,128)} fusion(f32[4,256,256]{2,1,0:T(8,128)} %bitcast.2, f32[4,256]{1,0:T(4,128)S(1)} %broadcast_maximum_fusion), kind=kLoop, calls=%fused_computation | loop fusion | flops 262144 | bytes 2101248 | tf_op jit(solution)/shard_map/div | solution.py:333
  72.3 0.0 copy-done
  (1 shorter events, 0.0 us)
Async XLA Ops:
  69.9 2.4 %copy-start = (f32[4,256]{1,0:T(4,128)}, f32[4,256]{1,0:T(4,128)S(1)}, u32[]{:S(2)}) copy-start(f32[4,256]{1,0:T(4,128)S(1)} %reshape.20) | copy-start | bytes 12292

commit v3 on v2

--- a/solution.py
+++ b/solution.py
@@ -31,7 +31,7 @@
     points, block_list, centroids, totals, mass,
     cents, arrived, list_out, list_in, wts,
     direct_out, far_out, near_in, merge_in, far_in, own_far, mass_out, mass_in,
-    local_sem, row_send, row_recv, list_send, list_recv,
+    local_sem, row_send, row_recv, list_send, list_recv, pass_send, pass_list_send,
     direct_send, far_send, near_recv, merge_recv, far_recv, mass_send, mass_recv,
 ):
     me = lax.axis_index("list")
@@ -63,34 +63,32 @@
     for k in range(1, n):
         peer = exclusive_or(me, k)
         pl.semaphore_signal(barrier, inc=1, device_id={"dp": dp, "list": peer}, device_id_type=MESH)
-        pl.semaphore_signal(barrier, inc=1, device_id={"dp": partner, "list": peer}, device_id_type=MESH)
     for k in range(1, dps):
         pl.semaphore_signal(barrier, inc=1, device_id={"dp": (dp + k) % dps, "list": me}, device_id_type=MESH)
     for o in range(n):
         list_out[o] = jnp.full((1, BLK), block_list[o], jnp.int32)
     list_in[0] = jnp.full((1, BLK), block_list[me], jnp.int32)
-    pl.semaphore_wait(barrier, 2 * (n - 1) + dps - 1)
+    pl.semaphore_wait(barrier, n - 1 + dps - 1)
 
     def route(i, odd):
         k = 2 * i + (core + odd) % 2
         owner = 2 * exclusive_or(chip, i) + odd
-        target = dp + odd * (home - dp)
-        return k, owner, target, k + n * odd * away
+        return k, owner
 
     def row_copy(i, odd):
-        k, owner, target, slot = route(i, odd)
-        return pltpu.make_async_remote_copy(
-            src_ref=points.at[owner], dst_ref=arrived.at[slot],
-            send_sem=row_send.at[k], recv_sem=row_recv.at[slot],
-            device_id={"dp": target, "list": owner}, device_id_type=MESH,
+        k, owner = route(i, odd)
+        return pltpu.make_async_remote_copy(
+            src_ref=points.at[owner], dst_ref=arrived.at[k],
+            send_sem=row_send.at[k], recv_sem=row_recv.at[k],
+            device_id={"dp": dp, "list": owner}, device_id_type=MESH,
         )
 
     def list_copy(i, odd):
-        k, owner, target, slot = route(i, odd)
-        return pltpu.make_async_remote_copy(
-            src_ref=list_out.at[owner], dst_ref=list_in.at[slot],
-            send_sem=list_send.at[k], recv_sem=list_recv.at[slot],
-            device_id={"dp": target, "list": owner}, device_id_type=MESH,
+        k, owner = route(i, odd)
+        return pltpu.make_async_remote_copy(
+            src_ref=list_out.at[owner], dst_ref=list_in.at[k],
+            send_sem=list_send.at[k], recv_sem=list_recv.at[k],
+            device_id={"dp": dp, "list": owner}, device_id_type=MESH,
         )
 
     def each_route(act):
@@ -99,9 +97,28 @@
                 if i:
                     act(i, odd)
                 else:
-                    @pl.when((core != odd) | (odd * away == 1))
+                    @pl.when(core != odd)
                     def _():
                         act(i, odd)
+
+    def forward_rows(k, source):
+        return pltpu.make_async_remote_copy(
+            src_ref=source, dst_ref=arrived.at[n + k],
+            send_sem=pass_send.at[k], recv_sem=row_recv.at[n + k],
+            device_id={"dp": partner, "list": me}, device_id_type=MESH,
+        )
+
+    def forward_list(k):
+        return pltpu.make_async_remote_copy(
+            src_ref=list_in.at[k], dst_ref=list_in.at[n + k],
+            send_sem=pass_list_send.at[k], recv_sem=list_recv.at[n + k],
+            device_id={"dp": partner, "list": me}, device_id_type=MESH,
+        )
+
+    @pl.when(idle)
+    def _():
+        forward_list(0).start()
+        forward_rows(0, points.at[me]).start()
 
     each_route(lambda i, odd: list_copy(i, odd).start())
     each_route(lambda i, odd: row_copy(i, odd).start())
@@ -132,6 +149,16 @@
 
     cent_copy.wait()
 
+    @pl.when(idle)
+    def _():
+        def pass_on(k, carry):
+            landed(k)
+            forward_list(k).start()
+            forward_rows(k, arrived.at[k]).start()
+            return carry
+
+        lax.fori_loop(1, n, pass_on, 0)
+
     @pl.when(jnp.logical_not(idle))
     def _():
         own_copy.wait()
@@ -248,6 +275,13 @@
     def _():
         totals[...] = jnp.zeros_like(totals)
         mass_out[...] = jnp.zeros_like(mass_out)
+
+        def passed(k, carry):
+            forward_list(k).wait_send()
+            forward_rows(k, points.at[me]).wait_send()
+            return carry
+
+        lax.fori_loop(0, n, passed, 0)
 
     mass[...] = mass_out[...]
     for k in range(1, dps):
@@ -320,7 +354,7 @@
             pltpu.VMEM((2 * SPLIT, PART, share), single),
             pltpu.VMEM((8, 128), single),
             pltpu.VMEM((dps - 1, 8, 128), single),
-            dma((2,)), dma((n,)), dma((2 * n,)), dma((n,)), dma((2 * n,)),
+            dma((2,)), dma((n,)), dma((2 * n,)), dma((n,)), dma((2 * n,)), dma((n,)), dma((n,)),
             dma((SPLIT,)), dma((2 * far,)), dma((SPLIT,)), dma((2 * far,)), dma((far,)),
             dma((dps - 1,)), dma((dps - 1,)),
         ],

time: 72.5 us -> 62.7 us (0.86)
  the two profiles are of different devices: /device:TPU:1 before, /device:TPU:8 now
where the time goes in v3:
time: 62.7 us; the launch traced here: 62.5 us
  Pallas kernels  58.7 us (94%)
  other arithmetic  2.41 us (4%)
  local copies, waits for them, and re-layouts  0.68 us (1%)
  between operations  0.64 us (1%)
    pallas_call x1, Pallas kernels, on_device(): pl.pallas_call(functools.partial(kernel, n, dps, share), out_shape=(jax.S...  58.7 us
    div x1, other arithmetic, on_device(): totals.reshape(LISTS_DEV, CENTS, share) / jnp.maximum(mass, 1.0)[..., None]  2.4 us

profile of v3, /device:TPU:8, one launch (start us, length us, event | category | flops | bytes accessed | tf_op | source)
XLA Modules:
  0.0 62.5 jit_solution(5015701524514046290)
XLA Ops:
  0.6 58.7 %shard_map.50 = (f32[1024,256]{1,0:T(8,128)}, f32[8,128]{1,0:T(8,128)}) custom-call(bf16[8,128,1024]{2,1,0:T(8,128)(2,1)} %bitcast.3, s32[8]{0:T(128)} %block_list.1, bf16[4,256,1024]{2,1,0:T(8,128)(2,1)} %centroids.1), custom_call_target="tpu_custom_call" | custom-call | flops 4294967296 | bytes 8388608 | tf_op jit(solution)/shard_map/pallas_call | solution.py:328
  59.4 0.7 %reshape.20 = f32[4,256]{1,0:T(4,128)S(1)} reshape(f32[8,128]{1,0:T(8,128)} %get-tuple-element.5) | data formatting | bytes 8192 | tf_op jit(solution)/shard_map/reshape | solution.py:366
  60.1 0.0 copy-start
  60.1 2.4 %broadcast_divide_fusion = f32[4,256,256]{2,1,0:T(8,128)} fusion(f32[4,256,256]{2,1,0:T(8,128)} %bitcast.2, f32[4,256]{1,0:T(4,128)S(1)} %broadcast_maximum_fusion), kind=kLoop, calls=%fused_computation | loop fusion | flops 262144 | bytes 2101248 | tf_op jit(solution)/shard_map/div | solution.py:367
  62.5 0.0 copy-done
  (1 shorter events, 0.0 us)
Async XLA Ops:
  60.1 2.4 %copy-start = (f32[4,256]{1,0:T(4,128)}, f32[4,256]{1,0:T(4,128)S(1)}, u32[]{:S(2)}) copy-start(f32[4,256]{1,0:T(4,128)S(1)} %reshape.20) | copy-start | bytes 12292
